TPU v7x, 128 devices: a whole 4x4x4 slice. The times are simulated.
128 devices in a mesh: freq: 8 (over x, y_lo), mat: 16 (over z, y_hi, core).
Axes of the slice: x: 4, y: 4 (y_hi: 2, y_lo: 2; y = y_hi * 2 + y_lo), z: 4, core: 2. Of those that a mesh axis runs over, the one named last changes fastest.
Arguments:
- traces: bfloat16 [2048, 64, 4096], P('freq', None, 'mat'), may hold values from -6 to 6
- reflection: bfloat16 [16, 2, 4096, 4096], P('freq', None, 'mat'), may hold values from -0.0625 to 0.0625
- onset: int32 [64, 4096], P(None, 'mat'), may hold values from 512 to 2047
Outputs:
- windowed: bfloat16 [2048, 64, 4096], P('freq', None, 'mat')
Inputs may be any that keep to these rules, and one draw needn't show every extreme that they name: onset sample of the direct arrival for each focal point and receiver.
All inputs are finite; a program needn't handle non-finite values.
Results may differ from a plain program's by a relative error of at most 0.0069.
Values may be sent and summed in bfloat16 or wider, within the bound.
A program may use at most 128 MiB of HBM per device.

v0:
```python
import math
import jax
import jax.numpy as jnp
from jax import lax
from jax.sharding import PartitionSpec as P


def forward_table(base_band, first_band, band_count, sample_time_count, sampling_interval):
    angular_freq_list = base_band + first_band + jnp.arange(band_count, dtype=jnp.int32)
    sample_moments = jnp.arange(sample_time_count, dtype=jnp.int32)
    phase_angles = (
        angular_freq_list[:, None] * sample_moments[None, :] % sampling_interval
    ).astype(jnp.float32) * (2.0 * math.pi / sampling_interval)
    factor = 1.0 / math.sqrt(sampling_interval)
    table = jnp.stack([jnp.cos(phase_angles) * factor, -jnp.sin(phase_angles) * factor], axis=1)
    return table.reshape(2 * band_count, sample_time_count).astype(jnp.bfloat16)


def inverse_table(
    base_band,
    first_band,
    band_count,
    earliest_sample_time,
    sample_time_count,
    sampling_interval,
    bands_total,
):
    angular_freq_list = base_band + first_band + jnp.arange(band_count, dtype=jnp.int32)
    sample_moments = earliest_sample_time + jnp.arange(sample_time_count, dtype=jnp.int32)
    phase_angles = (
        sample_moments[:, None] * angular_freq_list[None, :] % sampling_interval
    ).astype(jnp.float32) * (2.0 * math.pi / sampling_interval)
    factor = 1.0 / math.sqrt(bands_total)
    table = jnp.stack([jnp.cos(phase_angles) * factor, -jnp.sin(phase_angles) * factor], axis=2)
    return table.reshape(sample_time_count, 2 * band_count).astype(jnp.bfloat16)


def accumulate(reflection, panels):
    return jnp.einsum("kcpw,kdrw->kcpdr", panels, reflection, preferred_element_type=jnp.float32)


def on_device(traces, reflection, onset):
    temporal_rows, focal_count, recv_rows = traces.shape
    freq_devices = lax.axis_size("freq")
    sampling_interval = temporal_rows * freq_devices
    per_device = reflection.shape[0]
    bands_total = per_device * freq_devices
    base_band = sampling_interval // 16
    earliest_sample_time = lax.axis_index("freq") * temporal_rows
    gathered = lax.all_to_all(traces, "freq", split_axis=1, concat_axis=0, tiled=True)
    forward = forward_table(base_band, 0, bands_total, sampling_interval, sampling_interval)
    local_spectra = jnp.dot(
        forward, gathered.reshape(sampling_interval, -1), preferred_element_type=jnp.float32
    )
    local_spectra = local_spectra.astype(jnp.bfloat16).reshape(
        bands_total, 2, focal_count // freq_devices, recv_rows
    )
    spectra = lax.all_to_all(local_spectra, "freq", split_axis=0, concat_axis=2, tiled=True)
    products = accumulate(reflection, lax.all_gather(spectra, "mat", axis=3, tiled=True))
    real_part = products[:, 0, :, 0] - products[:, 1, :, 1]
    imag_part = products[:, 1, :, 0] + products[:, 0, :, 1]
    response = jnp.stack([real_part, imag_part], axis=1).astype(jnp.bfloat16)
    pieces = lax.all_gather(response, "freq", axis=0, tiled=True)
    piece_bands = pieces.shape[0]
    table = inverse_table(
        base_band,
        jnp.int32(0),
        piece_bands,
        earliest_sample_time,
        temporal_rows,
        sampling_interval,
        bands_total,
    )
    wavelet_trace = jnp.dot(
        table, pieces.reshape(2 * piece_bands, -1), preferred_element_type=jnp.float32
    )
    wavelet_trace = wavelet_trace.reshape(temporal_rows, focal_count, recv_rows)
    sample_moments = earliest_sample_time + jnp.arange(temporal_rows, dtype=jnp.int32)
    return jnp.where(sample_moments[:, None, None] < onset[None], wavelet_trace, 0.0).astype(
        jnp.bfloat16
    )


def solution(mesh):
    placed = (P("freq", None, "mat"), P("freq", None, "mat", None), P(None, "mat"))
    return jax.shard_map(
        on_device, mesh=mesh, in_specs=placed, out_specs=P("freq", None, "mat"), check_vma=False
    )
```

profile of v0, /device:TPU:0, one launch (start us, length us, event | category | flops | bytes accessed | tf_op | source)
XLA Modules:
  0.0 294.2 jit_solution(8987665596310700736)
XLA Ops:
  6.5 11.5 %copy.33 = bf16[256,64,256]{2,0,1:T(8,128)(2,1)} copy(bf16[256,64,256]{2,1,0:T(8,128)(2,1)} %param.3) | data formatting | bytes 16777216 | tf_op args[0]
  18.1 5.4 %all-to-all-start = ((bf16[256,64,256]{2,0,1:T(8,128)(2,1)}), bf16[256,64,256]{2,0,1:T(8,128)(2,1)}, u32[]{:S(2)}, u32[]{:S(2)}) async-start(bf16[256,64,256]{2,0,1:T(8,128)(2,1)} %copy.33), calls=%async_computation | async-start | bytes 16777216 | tf_op jit(solution)/shard_map/all_to_all | solution.py:50
  23.5 0.2 all-gather.3.cloned.1.call-start
  23.7 0.6 multiply_convert_fusion.1
  24.3 0.1 copy.32
  24.5 0.1 convert_element_type.60
  24.5 114.7 %all-to-all-done = bf16[256,64,256]{2,0,1:T(8,128)(2,1)} async-done(((bf16[256,64,256]{2,0,1:T(8,128)(2,1)}), bf16[256,64,256]{2,0,1:T(8,128)(2,1)}, u32[]{:S(2)}, u32[]{:S(2)}) %all-to-all-start) | async-done | bytes 8388640 | tf_op jit(solution)/shard_map/all_to_all | solution.py:50
  139.3 11.9 %copy.34 = bf16[256,8,8,256]{3,2,0,1:T(8,128)(2,1)} copy(bf16[256,8,8,256]{3,0,2,1:T(8,128)(2,1)} %bitcast) | data formatting | bytes 16777216 | tf_op jit(solution)/shard_map/all_to_all | solution.py:50
  151.2 10.3 %copy.46 = bf16[256,8,8,256]{3,1,2,0:T(8,128)(2,1)} copy(bf16[256,8,8,256]{3,2,1,0:T(8,128)(2,1)} %bitcast.60) | data formatting | bytes 16777216
  161.5 4.9 %convolution_convert_fusion = bf16[32,2048]{1,0:T(8,128)(2,1)S(1)} fusion(bf16[32,2048]{1,0:T(8,128)(2,1)S(1)} %convert_element_type.60, bf16[2048,2048]{1,0:T(8,128)(2,1)} %bitcast.59), kind=kOutput, calls=%fused_computation.3 | convolution fusion | flops 268500992 | bytes 8650752 | tf_op jit(solution)/shard_map/dot_general | solution.py:52
  166.4 0.0 copy-start
  166.5 9.7 %all_to_all.33 = bf16[16,2,8,256]{3,2,1,0:T(8,128)(2,1)S(1)} all-to-all(bf16[16,2,8,256]{3,2,1,0:T(8,128)(2,1)S(1)} %bitcast.64), channel_id=1, replica_groups=mesh['freq'=8,'mat'=16] {'freq'}, dimensions={0} | all-to-all | bytes 262144 | tf_op jit(solution)/shard_map/all_to_all | solution.py:58
  176.2 0.7 copy.57
  176.8 0.0 all-gather.3.cloned.1.call-update
  176.9 0.3 all-gather.5.cloned.1.call-start
  177.1 47.8 %all-gather.3.cloned.1.call-done = bf16[2,2,64,4096]{3,2,1,0:T(8,128)(2,1)} async-done(((bf16[2,2,64,256]{3,2,1,0:T(8,128)(2,1)}), bf16[2,2,64,4096]{3,2,1,0:T(8,128)(2,1)}) %all-gather.3.cloned.1.call-update) | async-done | bytes 2097168 | tf_op jit(solution)/shard_map/all_gather | solution.py:59
  224.9 6.9 %fusion = f32[2,2,64,2,256]{4,2,3,1,0:T(8,128)S(1)} fusion(bf16[2,2,256,4096]{3,2,1,0:T(8,128)(2,1)} %param.4, bf16[2,2,64,4096]{3,2,1,0:T(8,128)(2,1)} %all-gather.3.cloned.1.call-done), kind=kOutput, calls=%fused_computation.1 | convolution fusion | flops 1073741824 | bytes 11010048 | tf_op jit(solution)/shard_map/kcpw,kdrw->kcpdr/dot_general | solution.py:39
  231.9 0.7 pad_maximum_fusion.1
  232.6 0.0 all-gather.5.cloned.1.call-update
  232.6 0.2 multiply_convert_fusion.3
  232.8 37.0 %all-gather.5.cloned.1.call-done = bf16[16,2,64,256]{3,2,0,1:T(8,128)(2,1)} async-done(((bf16[2,2,64,256]{3,2,0,1:T(8,128)(2,1)}), bf16[16,2,64,256]{3,2,0,1:T(8,128)(2,1)}) %all-gather.5.cloned.1.call-update) | async-done | bytes 1048592 | tf_op jit(solution)/shard_map/all_gather | solution.py:63
  269.8 1.3 copy.38
  271.1 0.0 copy-done
  271.1 4.7 %select_convert_fusion = bf16[256,64,256]{2,0,1:T(8,128)(2,1)} fusion(bf16[256,32,1]{0,1,2:T(8,128)(2,1)S(1)} %reshape.327, s32[64,256]{1,0:T(8,128)S(1)} %copy-done, s32[256]{0:T(256)S(1)} %iota_add_fusion, bf16[4,8,64,256]{3,2,1,0:T(8,128)(2,1)S(1)} %bitcast.61), kind=kOutput, calls=%fused_computation | convolution fusion | flops 281018368 | bytes 9520128 | tf_op jit(solution)/shard_map/dot_general | solution.py:74
  275.8 11.5 %copy.40 = bf16[256,64,256]{2,1,0:T(8,128)(2,1)} copy(bf16[256,64,256]{2,0,1:T(8,128)(2,1)} %select_convert_fusion) | data formatting | bytes 16777216 | tf_op jit(solution)/shard_map/convert_element_type | solution.py:79
  (9 shorter events, 0.1 us)
Async XLA Ops:
  18.1 121.2 %all-to-all-start = ((bf16[256,64,256]{2,0,1:T(8,128)(2,1)}), bf16[256,64,256]{2,0,1:T(8,128)(2,1)}, u32[]{:S(2)}, u32[]{:S(2)}) async-start(bf16[256,64,256]{2,0,1:T(8,128)(2,1)} %copy.33), calls=%async_computation | async-start | bytes 16777216 | tf_op jit(solution)/shard_map/all_to_all | solution.py:50
  23.5 201.4 %all-gather.3.cloned.1.call-start = ((), (), s32[]{:S(2)}) async-start(), calls=%async_computation.2 | async-start | bytes 2228224 | tf_op jit(solution)/shard_map/all_gather | solution.py:59
  166.4 104.7 %copy-start = (s32[64,256]{1,0:T(8,128)S(1)}, s32[64,256]{1,0:T(8,128)}, u32[]{:S(2)}) copy-start(s32[64,256]{1,0:T(8,128)} %param.5) | copy-start | bytes 196612
  176.9 92.9 %all-gather.5.cloned.1.call-start = ((), (), s32[]{:S(2)}) async-start(), calls=%async_computation.3 | async-start | bytes 1179648 | tf_op jit(solution)/shard_map/all_gather | solution.py:63
Sparse Core Ops, SparseCore 0:
  177.0 47.8 all-gather.2
  232.7 37.0 all-gather.4
where the time goes:
time: 295 us; the launch traced here: 294 us
  waiting for transfers between devices  200 us (68%)
  local copies, waits for them, and re-layouts  47.5 us (16%)
  matrix products  16.5 us (6%)
  between operations  13.5 us (5%)
  blocking collectives  9.71 us (3%)
  starting transfers between devices  5.88 us (2%)
    all_to_all x1, waiting for transfers between devices, on_device(): lax.all_to_all(traces, 'freq', split_axis=1, concat_axis=0, tiled=True)  115 us
    all_gather x1, waiting for transfers between devices, on_device(): lax.all_gather(spectra, 'mat', axis=3, tiled=True)  47.8 us
    all_gather x1, waiting for transfers between devices, on_device(): pieces = lax.all_gather(response, 'freq', axis=0, tiled=True)  37 us
    unnamed x5, local copies, waits for them, and re-layouts  21.9 us
    all_to_all x1, local copies, waits for them, and re-layouts, on_device(): lax.all_to_all(traces, 'freq', split_axis=1, concat_axis=0, tiled=True)  11.9 us
    convert_element_type x1, local copies, waits for them, and re-layouts, on_device(): jnp.where(sample_moments[:, None, None] < onset[None], wavelet_trace, 0.0)  11.5 us
    all_to_all x1, blocking collectives, on_device(): lax.all_to_all(local_spectra, 'freq', split_axis=0, concat_axis=2, tiled=...  9.71 us
    dot_general x1, matrix products, accumulate(): jnp.einsum('kcpw,kdrw->kcpdr', panels, reflection, preferred_element_type...  6.94 us
  transfers between devices with their start and end apart: 3, of which 3 were waited for; matrix products, arithmetic and copies ran while one was open for 0% of the time, Pallas kernels for 0%

commit v1 on v0

--- a/solution.py
+++ b/solution.py
@@ -56,7 +56,12 @@
         bands_total, 2, focal_count // freq_devices, recv_rows
     )
     spectra = lax.all_to_all(local_spectra, "freq", split_axis=0, concat_axis=2, tiled=True)
-    products = accumulate(reflection, lax.all_gather(spectra, "mat", axis=3, tiled=True))
+    products = accumulate(
+        reflection,
+        jnp.concatenate(
+            lax.all_to_all(jnp.stack([spectra] * lax.axis_size("mat")), "mat", 0, 0), axis=3
+        ),
+    )
     real_part = products[:, 0, :, 0] - products[:, 1, :, 1]
     imag_part = products[:, 1, :, 0] + products[:, 0, :, 1]
     response = jnp.stack([real_part, imag_part], axis=1).astype(jnp.bfloat16)

time: 295 us -> 284 us (0.963)
  waiting for transfers between devices: 200 us -> 149 us
  blocking collectives: 9.71 us -> 46.7 us
  local copies, waits for them, and re-layouts: 47.5 us -> 50.7 us
    all_gather x1 -> x0, waiting for transfers between devices: 47.8 us -> none  [on_device(): lax.all_gather(spectra, 'mat', axis=3, tiled=True)]
    all_to_all x0 -> x1, blocking collectives: none -> 37 us  [on_device(): lax.all_to_all(jnp.stack([spectra] * lax.axis_size('mat')), 'mat', 0, 0)]
    reshape x0 -> x2, local copies, waits for them, and re-layouts: none -> 3.55 us  [on_device(): jnp.concatenate(lax.all_to_all(jnp.stack([spectra] * lax.axis_size('mat')...]
  transfers between devices with their start and end apart: 3 -> 2, of which waited for: 3 -> 2; matrix products, arithmetic and copies ran while one was open for 0% -> 0% of each run, Pallas kernels for 0% -> 0%
where the time goes in v1:
time: 284 us; the launch traced here: 283 us
  waiting for transfers between devices  149 us (52%)
  local copies, waits for them, and re-layouts  50.7 us (18%)
  blocking collectives  46.7 us (16%)
  matrix products  16.5 us (6%)
  between operations  13.5 us (5%)
  starting transfers between devices  5.61 us (2%)
    all_to_all x1, waiting for transfers between devices, on_device(): lax.all_to_all(traces, 'freq', split_axis=1, concat_axis=0, tiled=True)  115 us
    all_to_all x1, blocking collectives, on_device(): lax.all_to_all(jnp.stack([spectra] * lax.axis_size('mat')), 'mat', 0, 0)  37 us
    all_gather x1, waiting for transfers between devices, on_device(): pieces = lax.all_gather(response, 'freq', axis=0, tiled=True)  34 us
    unnamed x5, local copies, waits for them, and re-layouts  21.9 us
    all_to_all x1, local copies, waits for them, and re-layouts, on_device(): lax.all_to_all(traces, 'freq', split_axis=1, concat_axis=0, tiled=True)  11.9 us
    convert_element_type x1, local copies, waits for them, and re-layouts, on_device(): jnp.where(sample_moments[:, None, None] < onset[None], wavelet_trace, 0.0)  11.5 us
    all_to_all x1, blocking collectives, on_device(): lax.all_to_all(local_spectra, 'freq', split_axis=0, concat_axis=2, tiled=...  9.72 us
    dot_general x1, matrix products, accumulate(): jnp.einsum('kcpw,kdrw->kcpdr', panels, reflection, preferred_element_type...  6.94 us
  transfers between devices with their start and end apart: 2, of which 2 were waited for; matrix products, arithmetic and copies ran while one was open for 0% of the time, Pallas kernels for 0%

profile of v1, /device:TPU:0, one launch (start us, length us, event | category | flops | bytes accessed | tf_op | source)
XLA Modules:
  0.0 283.3 jit_solution(6931015237243575308)
XLA Ops:
  6.5 11.5 %copy.40 = bf16[256,64,256]{2,0,1:T(8,128)(2,1)} copy(bf16[256,64,256]{2,1,0:T(8,128)(2,1)} %param.3) | data formatting | bytes 16777216 | tf_op args[0]
  18.1 5.4 %all-to-all-start = ((bf16[256,64,256]{2,0,1:T(8,128)(2,1)}), bf16[256,64,256]{2,0,1:T(8,128)(2,1)}, u32[]{:S(2)}, u32[]{:S(2)}) async-start(bf16[256,64,256]{2,0,1:T(8,128)(2,1)} %copy.40), calls=%async_computation | async-start | bytes 16777216 | tf_op jit(solution)/shard_map/all_to_all | solution.py:50
  23.5 0.2 all-gather.2.cloned.1.call-start
  23.7 0.6 multiply_convert_fusion.1
  24.3 0.1 copy.39
  24.5 0.1 convert_element_type.60
  24.5 114.7 %all-to-all-done = bf16[256,64,256]{2,0,1:T(8,128)(2,1)} async-done(((bf16[256,64,256]{2,0,1:T(8,128)(2,1)}), bf16[256,64,256]{2,0,1:T(8,128)(2,1)}, u32[]{:S(2)}, u32[]{:S(2)}) %all-to-all-start) | async-done | bytes 8388640 | tf_op jit(solution)/shard_map/all_to_all | solution.py:50
  139.3 11.9 %copy.41 = bf16[256,8,8,256]{3,2,0,1:T(8,128)(2,1)} copy(bf16[256,8,8,256]{3,0,2,1:T(8,128)(2,1)} %bitcast) | data formatting | bytes 16777216 | tf_op jit(solution)/shard_map/all_to_all | solution.py:50
  151.2 10.3 %copy.54 = bf16[256,8,8,256]{3,1,2,0:T(8,128)(2,1)} copy(bf16[256,8,8,256]{3,2,1,0:T(8,128)(2,1)} %bitcast.61) | data formatting | bytes 16777216
  161.5 4.9 %convolution_convert_fusion = bf16[32,2048]{1,0:T(8,128)(2,1)S(1)} fusion(bf16[32,2048]{1,0:T(8,128)(2,1)S(1)} %convert_element_type.60, bf16[2048,2048]{1,0:T(8,128)(2,1)} %bitcast.60), kind=kOutput, calls=%fused_computation.3 | convolution fusion | flops 268500992 | bytes 8650752 | tf_op jit(solution)/shard_map/dot_general | solution.py:52
  166.5 9.7 %all_to_all.35 = bf16[16,2,8,256]{3,2,1,0:T(8,128)(2,1)S(1)} all-to-all(bf16[16,2,8,256]{3,2,1,0:T(8,128)(2,1)S(1)} %bitcast.66), channel_id=1, replica_groups=mesh['freq'=8,'mat'=16] {'freq'}, dimensions={0} | all-to-all | bytes 262144 | tf_op jit(solution)/shard_map/all_to_all | solution.py:58
  176.2 0.2 stack.16
  176.4 37.0 %all_to_all.36 = bf16[16,2,2,64,256]{4,3,2,1,0:T(8,128)(2,1)S(1)} all-to-all(bf16[16,2,2,64,256]{4,3,2,1,0:T(8,128)(2,1)S(1)} %stack.16), channel_id=1, replica_groups=mesh['freq'=8,'mat'=16] {'mat'}, dimensions={0} | all-to-all | bytes 4194304 | tf_op jit(solution)/shard_map/all_to_all | solution.py:62
  213.4 1.2 copy.43
  214.6 0.0 copy-start
  214.6 2.3 reshape.336
  217.0 6.9 %fusion = f32[2,2,64,2,256]{4,2,3,1,0:T(8,128)S(1)} fusion(bf16[2,2,256,4096]{3,2,1,0:T(8,128)(2,1)} %param.4, bf16[2,2,64,4096,1]{3,2,1,0,4:T(8,128)(2,1)} %reshape.336), kind=kOutput, calls=%fused_computation.1 | convolution fusion | flops 1073741824 | bytes 11010048 | tf_op jit(solution)/shard_map/kcpw,kdrw->kcpdr/dot_general | solution.py:39
  223.9 0.7 pad_maximum_fusion.1
  224.6 0.0 all-gather.2.cloned.1.call-update
  224.7 0.2 multiply_convert_fusion.3
  224.9 34.0 %all-gather.2.cloned.1.call-done = bf16[16,2,64,256]{3,2,0,1:T(8,128)(2,1)} async-done(((bf16[2,2,64,256]{3,2,0,1:T(8,128)(2,1)}), bf16[16,2,64,256]{3,2,0,1:T(8,128)(2,1)}) %all-gather.2.cloned.1.call-update) | async-done | bytes 1048592 | tf_op jit(solution)/shard_map/all_gather | solution.py:68
  258.9 1.3 copy.46
  260.2 0.0 copy-done
  260.2 4.7 %select_convert_fusion = bf16[256,64,256]{2,0,1:T(8,128)(2,1)} fusion(bf16[256,32,1]{0,1,2:T(8,128)(2,1)S(1)} %reshape.338, s32[64,256]{1,0:T(8,128)S(1)} %copy-done, s32[256]{0:T(256)S(1)} %iota_add_fusion, bf16[4,8,64,256]{3,2,1,0:T(8,128)(2,1)S(1)} %bitcast.63), kind=kOutput, calls=%fused_computation | convolution fusion | flops 281018368 | bytes 9520128 | tf_op jit(solution)/shard_map/dot_general | solution.py:79
  264.9 11.5 %copy.48 = bf16[256,64,256]{2,1,0:T(8,128)(2,1)} copy(bf16[256,64,256]{2,0,1:T(8,128)(2,1)} %select_convert_fusion) | data formatting | bytes 16777216 | tf_op jit(solution)/shard_map/convert_element_type | solution.py:84
  (10 shorter events, 0.1 us)
Async XLA Ops:
  18.1 121.2 %all-to-all-start = ((bf16[256,64,256]{2,0,1:T(8,128)(2,1)}), bf16[256,64,256]{2,0,1:T(8,128)(2,1)}, u32[]{:S(2)}, u32[]{:S(2)}) async-start(bf16[256,64,256]{2,0,1:T(8,128)(2,1)} %copy.40), calls=%async_computation | async-start | bytes 16777216 | tf_op jit(solution)/shard_map/all_to_all | solution.py:50
  23.5 235.4 %all-gather.2.cloned.1.call-start = ((), (), s32[]{:S(2)}) async-start(), calls=%async_computation.3 | async-start | bytes 1179648 | tf_op jit(solution)/shard_map/all_gather | solution.py:68
  214.6 45.6 %copy-start = (s32[64,256]{1,0:T(8,128)S(1)}, s32[64,256]{1,0:T(8,128)}, u32[]{:S(2)}) copy-start(s32[64,256]{1,0:T(8,128)} %param.5) | copy-start | bytes 196612
Sparse Core Ops, SparseCore 0:
  224.8 34.0 all-gather.1
